TPU v7x, 512 devices: a whole 4x4x16 slice. The times are simulated.
512 devices in a mesh: feat: 16 (over x, y), label: 32 (over z, core).
Axes of the slice: x: 4, y: 4, z: 16, core: 2. Of those that a mesh axis runs over, the one named last changes fastest.
Arguments:
- doc_blocks: int32 [384, 8], replicated, may hold values from 0 to 511, all different within a row
- doc_counts: int32 [384], replicated, may hold values from 1 to 8
- doc_values: bfloat16 [384, 8, 256], replicated, may hold values from 0.049804688 to 2
- pos_labels: int32 [384, 8], replicated, may hold values from 0 to 131071, as said below
- neg_labels: int32 [384, 24], replicated, may hold values from 0 to 131071, as said below
- in_weight: bfloat16 [512, 256, 2048], P('feat', None, 'label'), may hold values from -0.1875 to 0.1875
- out_weight: bfloat16 [131072, 2048], P(('feat', 'label')), may hold values from -0.29882812 to 0.29882812
Outputs:
- in_grad: bfloat16 [512, 256, 2048], P('feat', None, 'label')
- out_grad: bfloat16 [131072, 2048], P(('feat', 'label'))
Inputs may be any that keep to these rules, and one draw needn't show every extreme that they name: The ids in one row of doc_blocks are distinct. `pos_labels`: label c is held by the device of linear index c // 256 (feat index times the size of label plus label index); taken together with neg_labels, every device's labels are named by exactly 24 of the listed pairs. `neg_labels`: see pos_labels.
All inputs are finite; a program needn't handle non-finite values.
Results may differ from a plain program's by a relative error of at most 0.0065.
Values may be sent and summed in bfloat16 or wider, within the bound.
No kernel may reach another device: no remote copies, remote signals or barrier semaphores. Data moves between devices by JAX's collectives and lax.ppermute only.
A program may use at most 128 MiB of HBM per device.

v0:
```python
import jax
import jax.numpy as jnp
from jax import lax
from jax.sharding import PartitionSpec as P


def on_device(doc_blocks, doc_counts, doc_values, pos_labels, neg_labels, in_weight, out_weight):
    block_count, block_size, col_count = in_weight.shape
    doc_total, slot_count = doc_blocks.shape
    lab_count = out_weight.shape[0]
    feat_index = lax.axis_index("feat")
    label_index = lax.axis_index("label")
    label_size = lax.axis_size("label")
    first_block = feat_index * block_count
    local_ids = doc_blocks - first_block
    slots = jnp.arange(slot_count, dtype=jnp.int32)
    valid = slots[None, :] < doc_counts[:, None]
    picks = (
        local_ids[:, :, None] == jnp.arange(block_count, dtype=jnp.int32)[None, None, :]
    ) & valid[:, :, None]
    dense = jnp.einsum(
        "dkb,dkv->dbv", picks.astype(jnp.bfloat16), doc_values, preferred_element_type=jnp.float32
    )
    flat_inputs = dense.astype(jnp.bfloat16).reshape(doc_total, block_count * block_size)
    weight_flat = in_weight.reshape(block_count * block_size, col_count)
    partial_value = jnp.dot(flat_inputs, weight_flat, preferred_element_type=jnp.float32)
    pre = lax.psum(partial_value, "feat")
    hidden_part = jax.nn.silu(pre).astype(jnp.bfloat16)
    hidden = lax.all_gather(hidden_part, "label", axis=1, tiled=True)
    logit = lax.dot_general(
        hidden, out_weight, (((1,), (1,)), ((), ())), preferred_element_type=jnp.float32
    )
    device_index = feat_index * label_size + label_index
    first_label = device_index * lab_count
    local_labels = jnp.arange(lab_count, dtype=jnp.int32)[None, None, :] + first_label
    pos_count = jnp.sum((pos_labels[:, :, None] == local_labels).astype(jnp.float32), axis=1)
    neg_count = jnp.sum((neg_labels[:, :, None] == local_labels).astype(jnp.float32), axis=1)
    sig = jax.nn.sigmoid(logit)
    grad_pos = (sig - 1.0).astype(jnp.bfloat16).astype(jnp.float32)
    grad_neg = sig.astype(jnp.bfloat16).astype(jnp.float32)
    label_grad = (pos_count * grad_pos + neg_count * grad_neg).astype(jnp.bfloat16)
    out_grad = lax.dot_general(
        label_grad, hidden, (((0,), (0,)), ((), ())), preferred_element_type=jnp.float32
    ).astype(jnp.bfloat16)
    grad_terms = jnp.dot(label_grad, out_weight, preferred_element_type=jnp.float32)
    summed = lax.psum(grad_terms, ("feat", "label"))
    hidden_grad = lax.dynamic_slice_in_dim(summed, label_index * col_count, col_count, 1)
    gate = jax.nn.sigmoid(pre)
    pre_grad = (hidden_grad * gate * (1.0 + pre * (1.0 - gate))).astype(jnp.bfloat16)
    in_flat = lax.dot_general(
        flat_inputs, pre_grad, (((0,), (0,)), ((), ())), preferred_element_type=jnp.float32
    )
    in_grad = in_flat.astype(jnp.bfloat16).reshape(block_count, block_size, col_count)
    return (in_grad, out_grad)


def solution(mesh):
    placed = (P(), P(), P(), P(), P(), P("feat", None, "label"), P(("feat", "label"), None))
    return jax.shard_map(
        on_device,
        mesh=mesh,
        in_specs=placed,
        out_specs=(P("feat", None, "label"), P(("feat", "label"), None)),
        check_vma=False,
    )
```

profile of v0, /device:TPU:2, one launch (start us, length us, event | category | flops | bytes accessed | tf_op | source)
XLA Modules:
  0.0 713.3 jit_solution(14605121180167996716)
XLA Ops:
  7.2 0.0 copy-start
  7.2 0.0 all-reduce.3.cloned.1.call-start
  7.2 0.8 broadcast_subtract_fusion
  8.1 0.1 copy.14
  8.2 0.8 iota_compare_fusion.1
  9.0 0.0 copy-done
  9.0 0.0 copy-start.7
  9.0 3.8 convolution_convert_fusion.1
  12.9 2.6 copy-done.1
  15.5 7.4 %fusion.7 = f32[384,64]{0,1:T(8,128)} fusion(bf16[32,256,64]{1,2,0:T(8,128)(2,1)S(1)} %copy-done.7, bf16[384,32,256]{2,1,0:T(8,128)(2,1)S(1)} %convolution_convert_fusion.1), kind=kOutput, calls=%fused_computation.13 | convolution fusion | flops 402653184 | bytes 7438336 | tf_op jit(solution)/shard_map/dot_general | solution.py:26
  22.9 0.0 all-reduce.3.cloned.1.call-update
  22.9 0.0 all-gather.2.cloned.1.call-start
  23.0 116.3 %all-reduce.3.cloned.1.call-done = f32[384,64]{0,1:T(8,128)} async-done(((f32[384,64]{0,1:T(8,128)}), f32[384,64]{0,1:T(8,128)}) %all-reduce.3.cloned.1.call-update) | async-done | bytes 98320 | tf_op jit(solution)/shard_map/psum | solution.py:27
  139.3 1.6 multiply_convert_fusion.1
  140.8 0.0 all-gather.2.cloned.1.call-update
  140.9 0.0 all-reduce.5.cloned.1.call-start
  140.9 0.0 copy-done.5
  140.9 0.1 copy.17
  141.1 0.1 copy.15
  141.2 2.9 convert_reduce_fusion.1
  144.1 3.1 convert_reduce_fusion
  147.2 66.0 %all-gather.2.cloned.1.call-done = bf16[384,2048]{0,1:T(8,128)(2,1)} async-done(((bf16[384,64]{0,1:T(8,128)(2,1)}), bf16[384,2048]{0,1:T(8,128)(2,1)}) %all-gather.2.cloned.1.call-update) | async-done | bytes 1572880 | tf_op jit(solution)/shard_map/all_gather | solution.py:29
  213.2 2.2 add_convert_fusion
  215.4 2.4 fusion.15
  217.8 0.0 all-reduce.5.cloned.1.call-update
  217.8 0.0 copy-start.2
  217.9 0.0 copy-start.4
  217.9 12.9 %copy.20 = bf16[48,8,32,256]{3,1,2,0:T(8,128)(2,1)} copy(bf16[48,8,32,256]{3,2,1,0:T(8,128)(2,1)} %bitcast.18) | data formatting | bytes 12582912
  230.8 1.7 convolution_convert_fusion.2
  232.5 469.0 %all-reduce.5.cloned.1.call-done = f32[384,2048]{0,1:T(8,128)} async-done(((f32[384,2048]{0,1:T(8,128)}), f32[384,2048]{0,1:T(8,128)}) %all-reduce.5.cloned.1.call-update) | async-done | bytes 3145744 | tf_op jit(solution)/shard_map/psum | solution.py:46
  701.5 4.1 convolution_convert_fusion
  705.6 1.1 copy.26
  (10 shorter events, 0.0 us)
Async XLA Ops:
  7.2 1.8 copy-start
  7.2 132.1 %all-reduce.3.cloned.1.call-start = ((), (), s32[]{:S(2)}) async-start(), calls=%async_computation | async-start | bytes 196608 | tf_op jit(solution)/shard_map/psum | solution.py:27
  9.0 6.5 copy-start.7
  12.8 2.6 copy-start.1
  15.5 125.4 %copy-start.5 = (s32[384,24]{0,1:T(8,128)S(1)}, s32[384,24]{0,1:T(8,128)}, u32[]{:S(2)}) copy-start(s32[384,24]{0,1:T(8,128)} %param.11) | copy-start | bytes 110596
  15.5 125.6 %copy-start.6 = (s32[384,8]{0,1:T(8,128)S(1)}, s32[384,8]{0,1:T(8,128)}, u32[]{:S(2)}) copy-start(s32[384,8]{0,1:T(8,128)} %param.10) | copy-start | bytes 36868
  15.5 197.7 %copy-start.3 = (bf16[256,2048]{1,0:T(8,128)(2,1)S(1)}, bf16[256,2048]{1,0:T(8,128)(2,1)}, u32[]{:S(2)}) copy-start(bf16[256,2048]{1,0:T(8,128)(2,1)} %param.13) | copy-start | bytes 3145732
  22.9 190.2 %all-gather.2.cloned.1.call-start = ((), (), s32[]{:S(2)}) async-start(), calls=%async_computation.1 | async-start | bytes 1622016 | tf_op jit(solution)/shard_map/all_gather | solution.py:29
  140.9 560.7 %all-reduce.5.cloned.1.call-start = ((), (), s32[]{:S(2)}) async-start(), calls=%async_computation.2 | async-start | bytes 6291456 | tf_op jit(solution)/shard_map/psum | solution.py:46
  217.8 12.9 %copy-start.2 = (bf16[384,2048]{0,1:T(8,128)(2,1)S(1)}, bf16[384,2048]{0,1:T(8,128)(2,1)}, u32[]{:S(2)}) copy-start(bf16[384,2048]{0,1:T(8,128)(2,1)} %all-gather.2.cloned.1.call-done) | copy-start | bytes 4718596
  217.9 483.7 %copy-start.4 = (f32[384,64]{0,1:T(8,128)S(1)}, f32[384,64]{0,1:T(8,128)}, u32[]{:S(2)}) copy-start(f32[384,64]{0,1:T(8,128)} %all-reduce.3.cloned.1.call-done) | copy-start | bytes 294916
Sparse Core Ops, SparseCore 0:
  23.1 116.1 all-reduce.2
  141.6 71.4 all-gather.1
  219.3 482.1 all-reduce.4
where the time goes:
time: 713 us
  waiting for transfers between devices  651 us (91%)
  matrix products  21.7 us (3%)
  local copies, waits for them, and re-layouts  17 us (2%)
  between operations  13.9 us (2%)
  other arithmetic  9.17 us (1%)
    psum x1, waiting for transfers between devices, on_device(): summed = lax.psum(grad_terms, ('feat', 'label'))  469 us
    psum x1, waiting for transfers between devices, on_device(): pre = lax.psum(partial_value, 'feat')  116 us
    all_gather x1, waiting for transfers between devices, on_device(): hidden = lax.all_gather(hidden_part, 'label', axis=1, tiled=True)  66 us
    unnamed x19, local copies, waits for them, and re-layouts  15.8 us
  transfers between devices with their start and end apart: 3, of which 3 were waited for; matrix products, arithmetic and copies ran while one was open for 3% of the time, Pallas kernels for 0%

commit v1 on v0

--- a/solution.py
+++ b/solution.py
@@ -24,7 +24,7 @@
     flat_inputs = dense.astype(jnp.bfloat16).reshape(doc_total, block_count * block_size)
     weight_flat = in_weight.reshape(block_count * block_size, col_count)
     partial_value = jnp.dot(flat_inputs, weight_flat, preferred_element_type=jnp.float32)
-    pre = lax.psum(partial_value, "feat")
+    pre = jnp.sum(lax.all_gather(partial_value, "feat"), axis=0)
     hidden_part = jax.nn.silu(pre).astype(jnp.bfloat16)
     hidden = lax.all_gather(hidden_part, "label", axis=1, tiled=True)
     logit = lax.dot_general(

time: 713 us -> 660 us (0.926)
  waiting for transfers between devices: 651 us -> 597 us
    psum x1 -> x0, waiting for transfers between devices: 116 us -> none  [on_device(): pre = lax.psum(partial_value, 'feat')]
    all_gather x0 -> x1, waiting for transfers between devices: none -> 63.6 us  [on_device(): pre = jnp.sum(lax.all_gather(partial_value, 'feat'), axis=0)]
    unnamed x19 -> x18, local copies, waits for them, and re-layouts: 15.8 us -> 17.6 us
where the time goes in v1:
time: 660 us
  waiting for transfers between devices  597 us (90%)
  matrix products  21.7 us (3%)
  local copies, waits for them, and re-layouts  18.8 us (3%)
  between operations  13.9 us (2%)
  other arithmetic  8.51 us (1%)
    psum x1, waiting for transfers between devices, on_device(): summed = lax.psum(grad_terms, ('feat', 'label'))  468 us
    all_gather x1, waiting for transfers between devices, on_device(): hidden = lax.all_gather(hidden_part, 'label', axis=1, tiled=True)  64.9 us
    all_gather x1, waiting for transfers between devices, on_device(): pre = jnp.sum(lax.all_gather(partial_value, 'feat'), axis=0)  63.6 us
    unnamed x18, local copies, waits for them, and re-layouts  17.6 us
  transfers between devices with their start and end apart: 3, of which 3 were waited for; matrix products, arithmetic and copies ran while one was open for 3% of the time, Pallas kernels for 0%

profile of v1, /device:TPU:2, one launch (start us, length us, event | category | flops | bytes accessed | tf_op | source)
XLA Modules:
  0.0 659.7 jit_solution(10913370900829372124)
XLA Ops:
  7.2 0.0 copy-start
  7.2 0.0 all-gather.6.cloned.1.call-start
  7.2 0.8 broadcast_subtract_fusion
  8.1 0.1 copy.19
  8.2 0.8 iota_compare_fusion.1
  9.0 0.0 copy-start.6
  9.0 3.8 convolution_convert_fusion.1
  12.9 2.6 copy-done.1
  15.5 0.0 copy-done.6
  15.5 7.4 %fusion.7 = f32[384,64]{0,1:T(8,128)} fusion(bf16[32,256,64]{1,2,0:T(8,128)(2,1)S(1)} %copy-done.6, bf16[384,32,256]{2,1,0:T(8,128)(2,1)S(1)} %convolution_convert_fusion.1), kind=kOutput, calls=%fused_computation.14 | convolution fusion | flops 402653184 | bytes 7438336 | tf_op jit(solution)/shard_map/dot_general | solution.py:26
  22.9 0.0 all-gather.6.cloned.1.call-update
  22.9 0.0 all-gather.4.cloned.1.call-start
  23.0 63.6 %all-gather.6.cloned.1.call-done = f32[6144,64]{0,1:T(8,128)} async-done(((f32[384,64]{0,1:T(8,128)}), f32[6144,64]{0,1:T(8,128)}) %all-gather.6.cloned.1.call-update) | async-done | bytes 1572880 | tf_op jit(solution)/shard_map/all_gather | solution.py:27
  86.6 1.8 copy.25
  88.4 0.2 bitcast_reduce_fusion
  88.6 0.7 multiply_convert_fusion.1
  89.3 0.0 all-gather.4.cloned.1.call-update
  89.3 0.0 all-reduce.2.cloned.1.call-start
  89.4 0.1 copy.22
  89.5 0.0 copy-done.5
  89.5 0.1 copy.20
  89.6 2.9 convert_reduce_fusion.1
  92.5 3.1 convert_reduce_fusion
  95.6 64.9 %all-gather.4.cloned.1.call-done = bf16[384,2048]{0,1:T(8,128)(2,1)} async-done(((bf16[384,64]{0,1:T(8,128)(2,1)}), bf16[384,2048]{0,1:T(8,128)(2,1)}) %all-gather.4.cloned.1.call-update) | async-done | bytes 1572880 | tf_op jit(solution)/shard_map/all_gather | solution.py:29
  160.6 2.2 add_convert_fusion
  162.8 2.4 fusion.15
  165.2 0.0 all-reduce.2.cloned.1.call-update
  165.2 12.9 %copy.26 = bf16[48,8,32,256]{3,1,2,0:T(8,128)(2,1)} copy(bf16[48,8,32,256]{3,2,1,0:T(8,128)(2,1)} %bitcast.23) | data formatting | bytes 12582912
  178.1 1.7 convolution_convert_fusion.2
  179.9 468.1 %all-reduce.2.cloned.1.call-done = f32[384,2048]{0,1:T(8,128)} async-done(((f32[384,2048]{0,1:T(8,128)}), f32[384,2048]{0,1:T(8,128)}) %all-reduce.2.cloned.1.call-update) | async-done | bytes 3145744 | tf_op jit(solution)/shard_map/psum | solution.py:46
  648.0 4.1 convolution_convert_fusion
  652.1 1.1 copy.32
  (10 shorter events, 0.0 us)
Async XLA Ops:
  7.2 1.8 copy-start
  7.2 79.4 %all-gather.6.cloned.1.call-start = ((), (), s32[]{:S(2)}) async-start(), calls=%async_computation.2 | async-start | bytes 1671168 | tf_op jit(solution)/shard_map/all_gather | solution.py:27
  9.0 6.5 copy-start.6
  12.8 2.7 copy-start.1
  22.9 66.4 %copy-start.4 = (s32[384,24]{0,1:T(8,128)S(1)}, s32[384,24]{0,1:T(8,128)}, u32[]{:S(2)}) copy-start(s32[384,24]{0,1:T(8,128)} %param.11) | copy-start | bytes 110596
  22.9 66.6 %copy-start.5 = (s32[384,8]{0,1:T(8,128)S(1)}, s32[384,8]{0,1:T(8,128)}, u32[]{:S(2)}) copy-start(s32[384,8]{0,1:T(8,128)} %param.10) | copy-start | bytes 36868
  22.9 137.6 %all-gather.4.cloned.1.call-start = ((), (), s32[]{:S(2)}) async-start(), calls=%async_computation | async-start | bytes 1622016 | tf_op jit(solution)/shard_map/all_gather | solution.py:29
  86.6 74.0 %copy-start.3 = (bf16[256,2048]{1,0:T(8,128)(2,1)S(1)}, bf16[256,2048]{1,0:T(8,128)(2,1)}, u32[]{:S(2)}) copy-start(bf16[256,2048]{1,0:T(8,128)(2,1)} %param.13) | copy-start | bytes 3145732
  89.3 558.7 %all-reduce.2.cloned.1.call-start = ((), (), s32[]{:S(2)}) async-start(), calls=%async_computation.1 | async-start | bytes 6291456 | tf_op jit(solution)/shard_map/psum | solution.py:46
  165.2 12.9 %copy-start.2 = (bf16[384,2048]{0,1:T(8,128)(2,1)S(1)}, bf16[384,2048]{0,1:T(8,128)(2,1)}, u32[]{:S(2)}) copy-start(bf16[384,2048]{0,1:T(8,128)(2,1)} %all-gather.4.cloned.1.call-done) | copy-start | bytes 4718596
Sparse Core Ops, SparseCore 0:
  23.1 63.4 all-gather.5
  89.4 71.0 all-gather.3
  165.9 482.0 all-reduce.1

commit v2 on v0

--- a/solution.py
+++ b/solution.py
@@ -43,7 +43,7 @@
         label_grad, hidden, (((0,), (0,)), ((), ())), preferred_element_type=jnp.float32
     ).astype(jnp.bfloat16)
     grad_terms = jnp.dot(label_grad, out_weight, preferred_element_type=jnp.float32)
-    summed = lax.psum(grad_terms, ("feat", "label"))
+    summed = lax.psum(lax.psum(grad_terms, "feat"), "label")
     hidden_grad = lax.dynamic_slice_in_dim(summed, label_index * col_count, col_count, 1)
     gate = jax.nn.sigmoid(pre)
     pre_grad = (hidden_grad * gate * (1.0 + pre * (1.0 - gate))).astype(jnp.bfloat16)

time: 713 us -> 573 us (0.80)
  the two profiles are of different devices: /device:TPU:2 before, /device:TPU:1 now
where the time goes in v2:
time: 573 us
  waiting for transfers between devices  511 us (89%)
  matrix products  21.7 us (4%)
  local copies, waits for them, and re-layouts  17 us (3%)
  between operations  13.9 us (2%)
  other arithmetic  9.17 us (2%)
    psum x2, waiting for transfers between devices, on_device(): summed = lax.psum(lax.psum(grad_terms, 'feat'), 'label')  327 us
    psum x1, waiting for transfers between devices, on_device(): pre = lax.psum(partial_value, 'feat')  116 us
    all_gather x1, waiting for transfers between devices, on_device(): hidden = lax.all_gather(hidden_part, 'label', axis=1, tiled=True)  67 us
    unnamed x19, local copies, waits for them, and re-layouts  15.8 us
  transfers between devices with their start and end apart: 4, of which 4 were waited for; matrix products, arithmetic and copies ran while one was open for 4% of the time, Pallas kernels for 0%

profile of v2, /device:TPU:1, one launch (start us, length us, event | category | flops | bytes accessed | tf_op | source)
XLA Modules:
  0.0 573.1 jit_solution(6970861939728999574)
XLA Ops:
  7.2 0.0 copy-start
  7.2 0.0 all-reduce.4.cloned.1.call-start
  7.2 0.8 broadcast_subtract_fusion
  8.1 0.1 copy.14
  8.2 0.8 iota_compare_fusion.1
  9.0 0.0 copy-start.7
  9.0 3.8 convolution_convert_fusion.1
  12.9 2.6 copy-done.1
  15.5 7.4 %fusion.7 = f32[384,64]{0,1:T(8,128)} fusion(bf16[32,256,64]{1,2,0:T(8,128)(2,1)S(1)} %copy-done.7, bf16[384,32,256]{2,1,0:T(8,128)(2,1)S(1)} %convolution_convert_fusion.1), kind=kOutput, calls=%fused_computation.13 | convolution fusion | flops 402653184 | bytes 7438336 | tf_op jit(solution)/shard_map/dot_general | solution.py:26
  22.9 0.0 all-reduce.4.cloned.1.call-update
  22.9 0.0 all-gather.2.cloned.1.call-start
  23.0 116.5 %all-reduce.4.cloned.1.call-done = f32[384,64]{0,1:T(8,128)} async-done(((f32[384,64]{0,1:T(8,128)}), f32[384,64]{0,1:T(8,128)}) %all-reduce.4.cloned.1.call-update) | async-done | bytes 98320 | tf_op jit(solution)/shard_map/psum | solution.py:27
  139.5 1.6 multiply_convert_fusion.1
  141.0 0.0 all-gather.2.cloned.1.call-update
  141.1 0.0 all-reduce.6.cloned.1.call-start
  141.1 0.1 copy.17
  141.3 0.0 copy-done.6
  141.3 0.1 copy.15
  141.4 2.9 convert_reduce_fusion.1
  144.3 3.1 convert_reduce_fusion
  147.4 67.0 %all-gather.2.cloned.1.call-done = bf16[384,2048]{0,1:T(8,128)(2,1)} async-done(((bf16[384,64]{0,1:T(8,128)(2,1)}), bf16[384,2048]{0,1:T(8,128)(2,1)}) %all-gather.2.cloned.1.call-update) | async-done | bytes 1572880 | tf_op jit(solution)/shard_map/all_gather | solution.py:29
  214.4 2.2 add_convert_fusion
  216.7 2.4 fusion.15
  219.1 0.0 all-reduce.6.cloned.1.call-update
  219.1 0.2 all-reduce.8.cloned.1.call-start
  219.4 122.6 %all-reduce.6.cloned.1.call-done = f32[384,2048]{0,1:T(8,128)} async-done(((f32[384,2048]{0,1:T(8,128)}), f32[384,2048]{0,1:T(8,128)}) %all-reduce.6.cloned.1.call-update) | async-done | bytes 3145744 | tf_op jit(solution)/shard_map/psum | solution.py:46
  342.0 0.0 all-reduce.8.cloned.1.call-update
  342.0 12.9 %copy.20 = bf16[48,8,32,256]{3,1,2,0:T(8,128)(2,1)} copy(bf16[48,8,32,256]{3,2,1,0:T(8,128)(2,1)} %bitcast.18) | data formatting | bytes 12582912
  354.9 1.7 convolution_convert_fusion.2
  356.6 204.8 %all-reduce.8.cloned.1.call-done = f32[384,2048]{0,1:T(8,128)} async-done(((f32[384,2048]{0,1:T(8,128)}), f32[384,2048]{0,1:T(8,128)}) %all-reduce.8.cloned.1.call-update) | async-done | bytes 3145744 | tf_op jit(solution)/shard_map/psum | solution.py:46
  561.4 4.1 convolution_convert_fusion
  565.5 1.1 copy.26
  (13 shorter events, 0.0 us)
Async XLA Ops:
  7.2 1.8 copy-start
  7.2 132.3 %all-reduce.4.cloned.1.call-start = ((), (), s32[]{:S(2)}) async-start(), calls=%async_computation | async-start | bytes 196608 | tf_op jit(solution)/shard_map/psum | solution.py:27
  9.0 6.5 %copy-start.7 = (bf16[32,256,64]{1,2,0:T(8,128)(2,1)S(1)}, bf16[32,256,64]{1,2,0:T(8,128)(2,1)}, u32[]{:S(2)}) copy-start(bf16[32,256,64]{1,2,0:T(8,128)(2,1)} %param.12) | copy-start | bytes 3145732
  12.8 2.6 copy-start.1
  15.5 125.6 %copy-start.5 = (s32[384,24]{0,1:T(8,128)S(1)}, s32[384,24]{0,1:T(8,128)}, u32[]{:S(2)}) copy-start(s32[384,24]{0,1:T(8,128)} %param.11) | copy-start | bytes 110596
  15.5 125.8 %copy-start.6 = (s32[384,8]{0,1:T(8,128)S(1)}, s32[384,8]{0,1:T(8,128)}, u32[]{:S(2)}) copy-start(s32[384,8]{0,1:T(8,128)} %param.10) | copy-start | bytes 36868
  15.5 198.9 %copy-start.3 = (bf16[256,2048]{1,0:T(8,128)(2,1)S(1)}, bf16[256,2048]{1,0:T(8,128)(2,1)}, u32[]{:S(2)}) copy-start(bf16[256,2048]{1,0:T(8,128)(2,1)} %param.13) | copy-start | bytes 3145732
  22.9 191.5 %all-gather.2.cloned.1.call-start = ((), (), s32[]{:S(2)}) async-start(), calls=%async_computation.1 | async-start | bytes 1622016 | tf_op jit(solution)/shard_map/all_gather | solution.py:29
  141.1 200.9 %all-reduce.6.cloned.1.call-start = ((), (), s32[]{:S(2)}) async-start(), calls=%async_computation.2 | async-start | bytes 6291456 | tf_op jit(solution)/shard_map/psum | solution.py:46
  219.1 342.3 %all-reduce.8.cloned.1.call-start = ((), (), s32[]{:S(2)}) async-start(), calls=%async_computation.3 | async-start | bytes 6291456 | tf_op jit(solution)/shard_map/psum | solution.py:46
  342.0 12.9 %copy-start.2 = (bf16[384,2048]{0,1:T(8,128)(2,1)S(1)}, bf16[384,2048]{0,1:T(8,128)(2,1)}, u32[]{:S(2)}) copy-start(bf16[384,2048]{0,1:T(8,128)(2,1)} %all-gather.2.cloned.1.call-done) | copy-start | bytes 4718596
  342.0 219.4 %copy-start.4 = (f32[384,64]{0,1:T(8,128)S(1)}, f32[384,64]{0,1:T(8,128)}, u32[]{:S(2)}) copy-start(f32[384,64]{0,1:T(8,128)} %all-reduce.4.cloned.1.call-done) | copy-start | bytes 294916
Sparse Core Ops, SparseCore 0:
  23.1 116.3 all-reduce.3
  141.8 72.5 all-gather.1
  219.3 122.6 all-reduce.5
  344.3 217.0 all-reduce.7
